TPU v7x, 32 devices: a whole 2x2x4 slice. The times are simulated.
32 devices in a mesh: seq: 8 (over z, x), tile: 4 (over y, core).
Axes of the slice: x: 2, y: 2, z: 4, core: 2. Of those that a mesh axis runs over, the one named last changes fastest.
Arguments:
- query_feat: float32 [1536, 4096], P('seq', 'tile'), may hold values from -6 to 6
- key_feat: float32 [1536, 4096], P('seq', 'tile'), may hold values from -6 to 6
- value_feat: float32 [1536, 4096], P('seq', 'tile'), may hold values from -6 to 6
- short_filter: float32 [3, 7, 4096], P(None, None, 'tile'), may hold values from -3 to 3
- medium_filter: float32 [128, 4096], P(None, 'tile'), may hold values from -0.6 to 0.6
- out_weight: bfloat16 [4096, 4096], P('tile'), may hold values from -0.09375 to 0.09375
- cotangent: bfloat16 [1536, 4096], P('seq', 'tile'), may hold values from -6 to 6
Outputs:
- block_out: float32 [1536, 4096], P('seq', 'tile')
- grad_query: float32 [1536, 4096], P('seq', 'tile')
- grad_key: float32 [1536, 4096], P('seq', 'tile')
- grad_value: float32 [1536, 4096], P('seq', 'tile')
- grad_short: float32 [3, 7, 4096], P(None, None, 'tile')
- grad_medium: float32 [128, 4096], P(None, 'tile')
All inputs are finite; a program needn't handle non-finite values.
Results may differ from a plain program's by a relative error of at most 0.0029.
Values may be sent and summed in bfloat16 or wider, within the bound.
A program may use at most 64 MiB of HBM per device.

v0:
```python
import functools
import math

import jax
import jax.numpy as jnp
import ml_dtypes
import numpy as np
from jax import lax
from jax.experimental import pallas as pl
from jax.experimental.pallas import tpu as pltpu
from jax.sharding import PartitionSpec as P

MESH = pl.DeviceIdType.MESH
F32 = jnp.float32
BF16 = jnp.bfloat16
LANES = 128
WIDE = 512
EDGE = 8


def split_const(matrix, wide=True):
    hi = matrix.astype(np.float32).astype(ml_dtypes.bfloat16)
    lo = (matrix - hi.astype(np.float64)).astype(np.float32).astype(ml_dtypes.bfloat16)
    return np.concatenate([hi, lo, hi] if wide else [hi, lo], axis=1)


def dft_consts(rows, taps):
    size = rows + taps
    theta = 2.0 * np.pi * (np.arange(size // 2) + 0.5) / size

    def forward(first, last, wide=True):
        angle = theta[:, None] * np.arange(first, last)[None, :]
        return split_const(np.concatenate([np.cos(angle), -np.sin(angle)], axis=0), wide)

    def inverse(first, last):
        angle = np.arange(first, last)[:, None] * theta[None, :]
        return split_const(np.concatenate([np.cos(angle), -np.sin(angle)], axis=1) * (2.0 / size))

    return (
        forward(0, taps),
        forward(taps, size),
        forward(0, rows),
        forward(rows, size, False),
        inverse(taps, size),
        inverse(0, rows),
        inverse(-taps, 0),
    )


def mm(a, b):
    return jnp.dot(a, b, preferred_element_type=F32)


def dft_wide(matrix, x):
    hi = x.astype(BF16)
    lo = (x - hi.astype(F32)).astype(BF16)
    return mm(matrix[...], jnp.concatenate([hi, hi, lo], axis=0))


def dft_half(matrix, x):
    return mm(matrix[:, :2 * x.shape[0]], jnp.concatenate([x, x], axis=0))


def times(a, b):
    half = a.shape[0] // 2
    ar, ai, br, bi = a[:half], a[half:], b[:half], b[half:]
    return jnp.concatenate([ar * br - ai * bi, ar * bi + ai * br], axis=0)


def conj_times(a, b):
    half = a.shape[0] // 2
    ar, ai, br, bi = a[:half], a[half:], b[:half], b[half:]
    return jnp.concatenate([ar * br + ai * bi, ar * bi - ai * br], axis=0)


def low_bit(r):
    return (r & -r).bit_length() - 1


def kernel(
    n_seq, n_tile, n_own, scale,
    xq, xk, xv, cot, weight, sf_in, mf_in, fw_taps_in, fw_tail_in, fw_head_in, fw_after_in, inv_tail_in,
    inv_head_in, inv_taps_in,
    out_ref, gq_ref, gk_ref, gv_ref, gs_ref, gm_ref,
    sf, mf, fw_taps, fw_tail, fw_head, fw_after, inv_tail, inv_head, inv_taps,
    xe, wv, cotv, hspec, gspec, vspec, ks, vs, qs, gated, gg, gmix, ge, gout, part,
    ghalo_s, ghalo_r, mhalo_s, mhalo_r, psend, precv, msend, mrecv, mall, ssend, srecv, sall,
    t_sem, x_sem, w_sem, c_sem, xh_ss, xh_rs, ca_ss, ca_rs, gh_ss, gh_rs, mh_ss, mh_rs,
    eh_ss, eh_rs, p_ss, p_rs, m_ss, m_rs, ma_ss, ma_rs, s_ss, s_rs, sa_ss, sa_rs,
):
    rows, width = ks.shape
    taps = mf.shape[0]
    short = sf.shape[1]
    block = cotv.shape[2]
    bits = n_tile.bit_length() - 1
    x_refs = (xq, xk, xv)
    me = lax.axis_index("seq")
    tile = lax.axis_index("tile")

    def flip(k):
        return tile + (1 << k) - (2 << k) * ((tile // (1 << k)) % 2)

    def relative(r):
        index = tile * 0
        for k in range(bits):
            bit = (tile // (1 << k)) % 2
            index = index + (1 << k) * ((1 - bit) if (r >> k) & 1 else bit)
        return index

    def to_seq(src, dst, send, recv, index):
        return pltpu.make_async_remote_copy(src, dst, send, recv, device_id={"seq": index}, device_id_type=MESH)

    def to_tile(src, dst, send, recv, k):
        return pltpu.make_async_remote_copy(src, dst, send, recv, device_id={"tile": flip(k)}, device_id_type=MESH)

    def lanes(c, size):
        return pl.ds(pl.multiple_of(c * size, size), size)

    def over(size, body):
        def step(c, carry):
            body(c, lanes(c, size))
            return carry
        lax.fori_loop(0, width // size, step, 0)

    def parts(c):
        return [pl.ds(pl.multiple_of(c * WIDE + p * LANES, LANES), LANES) for p in range(WIDE // LANES)]

    table_pairs = (
        (mf_in, mf), (fw_taps_in, fw_taps), (sf_in, sf), (fw_tail_in, fw_tail), (fw_head_in, fw_head),
        (fw_after_in, fw_after), (inv_tail_in, inv_tail), (inv_head_in, inv_head), (inv_taps_in, inv_taps),
    )
    tables = [pltpu.make_async_copy(pair[0], pair[1], t_sem.at[i]) for i, pair in enumerate(table_pairs)]
    for copy in tables[:3]:
        copy.start()
    x_copies = [pltpu.make_async_copy(x_refs[i], xe.at[i, pl.ds(EDGE, rows)], x_sem.at[i]) for i in range(3)]
    for copy in x_copies:
        copy.start()
    own_cot = pltpu.make_async_copy(cot, cotv.at[0], c_sem)
    own_cot.start()
    for copy in tables[3:]:
        copy.start()
    w_copies = []
    for r in range(n_tile):
        columns = pl.ds(pl.multiple_of(relative(r) * block, block), block)
        w_copies.append(pltpu.make_async_copy(weight.at[:, columns], wv.at[r], w_sem.at[r]))
        w_copies[-1].start()

    barrier = pltpu.get_barrier_semaphore()

    def greet(d, carry):
        pl.semaphore_signal(barrier, inc=1, device_id={"seq": (me + d) % n_seq}, device_id_type=MESH)
        return carry
    lax.fori_loop(1, n_seq, greet, 0)
    for k in range(bits):
        pl.semaphore_signal(barrier, inc=1, device_id={"tile": flip(k)}, device_id_type=MESH)
    pl.semaphore_wait(barrier, n_seq - 1 + bits)

    has_next = me < n_seq - 1
    has_prev = me > 0
    nxt = (me + 1) % n_seq
    prv = (me + n_seq - 1) % n_seq

    x_halo = [
        to_seq(x_refs[i].at[pl.ds(rows - EDGE, EDGE)], xe.at[i, pl.ds(0, EDGE)], xh_ss.at[i], xh_rs.at[i], nxt)
        for i in range(3)
    ]

    @pl.when(has_next)
    def _():
        for i in (1, 2, 0):
            x_halo[i].start()

    gather = {}
    for k in reversed(range(bits)):
        gather[1 << k] = to_tile(cot, cotv.at[1 << k], ca_ss.at[1 << k], ca_rs.at[1 << k], k)
        gather[1 << k].start()

    @pl.when(jnp.logical_not(has_prev))
    def _():
        for i in range(3):
            xe[i, pl.ds(0, EDGE), :] = jnp.zeros((EDGE, width), F32)
        ghalo_r[...] = jnp.zeros_like(ghalo_r)

    @pl.when(jnp.logical_not(has_next))
    def _():
        for i in range(3):
            ge[i, pl.ds(rows, EDGE), :] = jnp.zeros((EDGE, width), F32)
        mhalo_r[...] = jnp.zeros_like(mhalo_r)

    for copy in tables[:3]:
        copy.wait()

    for copy in x_copies:
        copy.wait()

    @pl.when(has_prev)
    def _():
        for i in range(3):
            x_halo[i].wait_recv()

    def short_conv(i, ls):
        total = sf[i, pl.ds(0, 1), ls] * xe[i, pl.ds(EDGE, rows), ls]
        for j in range(1, short):
            total = total + sf[i, pl.ds(j, 1), ls] * xe[i, pl.ds(EDGE - j, rows), ls]
        return total

    def key_value(c, ls):
        hspec[:, ls] = dft_wide(fw_taps, mf[:, ls])
        for sub in parts(c):
            k_rows = short_conv(1, sub)
            ks[:, sub] = k_rows
            v_rows = short_conv(2, sub)
            vs[:, sub] = v_rows
            product = k_rows * v_rows
            gated[:, sub] = product
            ghalo_s[:, sub] = product[rows - taps:].astype(BF16)
    over(WIDE, key_value)

    ghalo = to_seq(ghalo_s, ghalo_r, gh_ss, gh_rs, nxt)

    @pl.when(has_next)
    def _():
        ghalo.start()

    for copy in tables[3:]:
        copy.wait()

    for r in range(n_tile):
        if r == 0:
            own_cot.wait()
        else:
            gather[r].wait_recv()
            for k in reversed(range(low_bit(r))):
                slot = r + (1 << k)
                gather[slot] = to_tile(cotv.at[r], cotv.at[slot], ca_ss.at[slot], ca_rs.at[slot], k)
                gather[slot].start()
        w_copies[r].wait()

        def grad_block(c, ls, r=r):
            term = lax.dot_general(
                cotv[r], wv[r, ls, :], (((1,), (1,)), ((), ())), preferred_element_type=F32
            )
            if r > 0:
                term = term + gg[:, ls]
            else:
                gspec[:, ls] = dft_wide(fw_tail, gated[:, ls])
                for sub in parts(c):
                    qs[:, sub] = short_conv(0, sub)
            gg[:, ls] = term
            if r == n_tile - 1:
                grad_mixed = term * qs[:, ls]
                gmix[:, ls] = grad_mixed
                mhalo_s[:, ls] = grad_mixed[:taps].astype(BF16)
        over(WIDE, grad_block)

    mhalo = to_seq(mhalo_s, mhalo_r, mh_ss, mh_rs, prv)

    @pl.when(has_prev)
    def _():
        mhalo.start()

    @pl.when(has_prev)
    def _():
        ghalo.wait_recv()

    per_wide = WIDE // LANES

    def mixed_rows(c, ls):
        v_spec = dft_wide(fw_head, gmix[:, ls])
        vspec[:, ls] = v_spec
        spectrum = gspec[:, ls] + dft_half(fw_taps, ghalo_r[:, ls])
        mixed = dft_wide(inv_tail, times(spectrum, hspec[:, ls]))
        gout[:, ls] = (qs[:, ls] * mixed).astype(BF16)
        ge[0, pl.ds(0, rows), ls] = gg[:, ls] * mixed
        terms = (dft_wide(inv_taps, conj_times(spectrum, v_spec)) * scale).astype(BF16)
        for p in range(per_wide):
            msend[c * per_wide + p] = terms[:, p * LANES:(p + 1) * LANES]
    over(WIDE, mixed_rows)

    e_halo = [
        to_seq(ge.at[i, pl.ds(0, EDGE)], ge.at[i, pl.ds(rows, EDGE)], eh_ss.at[i], eh_rs.at[i], prv) for i in range(3)
    ]

    @pl.when(has_prev)
    def _():
        e_halo[0].start()

    scatter = {}

    def project(r, beside=None):
        def body(c, carry):
            ds = lanes(c, WIDE)
            if beside is not None:
                beside(c, ds)
            term = mm(gout[...], wv[r, :, ds])
            if r & 1:
                psend[r, :, ds] = term.astype(BF16)
            else:
                part[r, :, ds] = term
            return carry
        lax.fori_loop(0, block // WIDE, body, 0)

    def send_sum(r):
        k = low_bit(r)
        scatter[r] = to_tile(psend.at[r], precv.at[r], p_ss.at[r], p_rs.at[r], k)
        scatter[r].start()

    def owner_copy(send, recv, ss, rs, d):
        return to_seq(send.at[(me + d) % n_seq], recv.at[d], ss.at[d], rs.at[d], (me + d) % n_seq)

    def if_owner(index, body):
        if n_own == n_seq:
            body()
        else:
            pl.when(index < n_own)(body)

    def peers(body):
        def step(d, carry):
            body(d)
            return carry
        lax.fori_loop(1, n_seq, step, 0)

    def to_owners(send, recv, ss, rs):
        peers(lambda d: if_owner((me + d) % n_seq, lambda: owner_copy(send, recv, ss, rs, d).start()))

    def from_owner_copy(full, ss, rs, d):
        return to_seq(full.at[me], full.at[me], ss.at[d], rs.at[d], (me + d) % n_seq)

    def owner_sum(send, recv, ss, rs, full, f_ss, f_rs):
        def body():
            def add(d, total):
                owner_copy(send, recv, ss, rs, d).wait_recv()
                return total + recv[d].astype(F32)
            total = lax.fori_loop(1, n_seq, add, send[me].astype(F32))
            full[me] = total.astype(full.dtype)
            peers(lambda d: from_owner_copy(full, f_ss, f_rs, d).start())
        if_owner(me, body)

    def from_owners(full, ss, rs):
        def wait(d):
            source = (me + n_seq - d) % n_seq
            if_owner(source, lambda: to_seq(full.at[source], full.at[source], ss.at[d], rs.at[d], source).wait_recv())
        peers(wait)

    def end_sends(send, recv, ss, rs, full, f_ss, f_rs):
        peers(lambda d: if_owner((me + d) % n_seq, lambda: owner_copy(send, recv, ss, rs, d).wait_send()))
        if_owner(me, lambda: peers(lambda d: from_owner_copy(full, f_ss, f_rs, d).wait_send()))

    medium_set = (msend, mrecv, m_ss, m_rs, mall, ma_ss, ma_rs)
    short_set = (ssend, srecv, s_ss, s_rs, sall, sa_ss, sa_rs)
    to_owners(*medium_set[:4])

    def add_sums(r, first, last):
        total = part[r]
        for k in range(first, last):
            scatter[r + (1 << k)].wait_recv()
            total = total + precv[r + (1 << k)].astype(F32)
        return total

    def step_sums(k):
        for r in range(1 << k, n_tile, 2 << k):
            psend[r] = add_sums(r, 0, k).astype(BF16)
            send_sum(r)

    def short_grad(i, c):
        for p, sub in enumerate(parts(c)):
            g_rows = ge[i, pl.ds(0, rows), sub] * scale
            for j in range(short):
                ssend[c * per_wide + p, pl.ds(i * EDGE + j, 1), :] = jnp.sum(
                    g_rows * xe[i, pl.ds(EDGE - j, rows), sub], axis=0, keepdims=True
                )
            for j in range(short, EDGE):
                ssend[c * per_wide + p, pl.ds(i * EDGE + j, 1), :] = jnp.zeros((1, LANES), F32)

    outs = (gq_ref, gk_ref, gv_ref)

    def feature_grad(i, c):
        for sub in parts(c):
            total = sf[i, pl.ds(0, 1), sub] * ge[i, pl.ds(0, rows), sub]
            for j in range(1, short):
                total = total + sf[i, pl.ds(j, 1), sub] * ge[i, pl.ds(j, rows), sub]
            outs[i][:, sub] = total

    for r in range(n_tile - 1, 0, -2):
        project(r, (lambda c, ls: short_grad(0, c)) if r == n_tile - 1 else None)
        send_sum(r)

    @pl.when(has_next)
    def _():
        mhalo.wait_recv()
        e_halo[0].wait_recv()

    def product_rows(c, ls):
        spectrum = vspec[:, ls] + dft_half(fw_after, mhalo_r[:, ls])
        grad_prod = dft_wide(inv_head, conj_times(hspec[:, ls], spectrum))
        ge[1, pl.ds(0, rows), ls] = grad_prod * vs[:, ls]
        ge[2, pl.ds(0, rows), ls] = grad_prod * ks[:, ls]
        feature_grad(0, c)

    project(2 % n_tile, product_rows)

    @pl.when(has_prev)
    def _():
        e_halo[1].start()
        e_halo[2].start()

    for r in range(4, n_tile, 2):
        project(r)
    for k in range(1, bits):
        step_sums(k)
    owner_sum(*medium_set)

    def last_short(c, ls):
        short_grad(1, c)
        short_grad(2, c)

    project(0, last_short)
    to_owners(*short_set[:4])

    @pl.when(has_next)
    def _():
        e_halo[1].wait_recv()
        e_halo[2].wait_recv()

    def last_features(c, ls):
        feature_grad(1, c)
        feature_grad(2, c)
    over(WIDE, last_features)

    owner_sum(*short_set)
    out_ref[...] = add_sums(0, 0, bits)

    from_owners(mall, ma_ss, ma_rs)
    from_owners(sall, sa_ss, sa_rs)

    for o in range(n_own):
        columns = slice(o * LANES, (o + 1) * LANES)
        gm_ref[:, columns] = mall[o].astype(F32)
        for i in range(3):
            gs_ref[i, :, columns] = sall[o, i * EDGE:i * EDGE + short]

    end_sends(*medium_set)
    end_sends(*short_set)
    for r in range(1, n_tile):
        gather[r].wait_send()
        scatter[r].wait_send()

    @pl.when(has_next)
    def _():
        for i in range(3):
            x_halo[i].wait_send()
        ghalo.wait_send()

    @pl.when(has_prev)
    def _():
        for i in range(3):
            e_halo[i].wait_send()
        mhalo.wait_send()


def write_results(*refs):
    count = len(refs) // 2
    sems = refs[-1]
    copies = [pltpu.make_async_copy(refs[i], refs[count + i], sems.at[i]) for i in range(count)]
    for copy in copies:
        copy.start()
    for copy in copies:
        copy.wait()


def shards(n_seq, n_tile, query_feat, key_feat, value_feat, short_filter, medium_filter, out_weight, cotangent):
    rows, width = query_feat.shape
    short = short_filter.shape[1]
    taps = medium_filter.shape[0]
    block = cotangent.shape[1]
    size = rows + taps
    n_own = width // LANES
    assert width == block and n_tile >= 4
    assert n_own <= n_seq and short <= EDGE and rows >= taps
    scale = 1.0 / math.sqrt(n_seq * rows)
    consts = dft_consts(rows, taps)
    hbm = pl.BlockSpec(memory_space=pltpu.HBM)
    vmem = pl.BlockSpec(memory_space=pltpu.VMEM)
    dma = pltpu.SemaphoreType.DMA
    results = pl.pallas_call(
        functools.partial(kernel, n_seq, n_tile, n_own, scale),
        out_shape=(
            pltpu.VMEM((rows, block), F32),
            pltpu.VMEM((rows, width), F32),
            pltpu.VMEM((rows, width), F32),
            pltpu.VMEM((rows, width), F32),
            pltpu.VMEM(short_filter.shape, F32),
            pltpu.VMEM(medium_filter.shape, F32),
        ),
        in_specs=[hbm] * 14,
        out_specs=[vmem] * 6,
        scratch_shapes=[
            pltpu.VMEM(short_filter.shape, F32),
            pltpu.VMEM(medium_filter.shape, F32),
            *[pltpu.VMEM(c.shape, BF16) for c in consts],
            pltpu.VMEM((3, rows + EDGE, width), F32),
            pltpu.VMEM((n_tile, width, block), BF16),
            pltpu.VMEM((n_tile, rows, block), BF16),
            pltpu.VMEM((size, width), F32),
            pltpu.VMEM((size, width), F32),
            pltpu.VMEM((size, width), F32),
            pltpu.VMEM((rows, width), F32),
            pltpu.VMEM((rows, width), F32),
            pltpu.VMEM((rows, width), F32),
            pltpu.VMEM((rows, width), F32),
            pltpu.VMEM((rows, width), F32),
            pltpu.VMEM((rows, width), F32),
            pltpu.VMEM((3, rows + EDGE, width), F32),
            pltpu.VMEM((rows, width), BF16),
            pltpu.VMEM((n_tile, rows, block), F32),
            pltpu.VMEM((taps, width), BF16),
            pltpu.VMEM((taps, width), BF16),
            pltpu.VMEM((taps, width), BF16),
            pltpu.VMEM((taps, width), BF16),
            pltpu.VMEM((n_tile, rows, block), BF16),
            pltpu.VMEM((n_tile, rows, block), BF16),
            pltpu.VMEM((n_own, taps, LANES), BF16),
            pltpu.VMEM((n_seq, taps, LANES), BF16),
            pltpu.VMEM((n_own, taps, LANES), BF16),
            pltpu.VMEM((n_own, 3 * EDGE, LANES), F32),
            pltpu.VMEM((n_seq, 3 * EDGE, LANES), F32),
            pltpu.VMEM((n_own, 3 * EDGE, LANES), F32),
            dma((9,)),
            dma((3,)),
            dma((n_tile,)),
            dma,
            dma((3,)),
            dma((3,)),
            dma((n_tile,)),
            dma((n_tile,)),
            dma,
            dma,
            dma,
            dma,
            dma((3,)),
            dma((3,)),
            dma((n_tile,)),
            dma((n_tile,)),
            *[dma((n_seq,)) for _ in range(8)],
        ],
        compiler_params=pltpu.CompilerParams(
            collective_id=0, has_side_effects=True, vmem_limit_bytes=60 * 1024 * 1024
        ),
    )(
        query_feat, key_feat, value_feat, cotangent, out_weight, short_filter, medium_filter,
        *[jnp.asarray(c) for c in consts],
    )
    return pl.pallas_call(
        write_results,
        out_shape=tuple(jax.ShapeDtypeStruct(r.shape, r.dtype) for r in results),
        in_specs=[pl.BlockSpec(memory_space=pl.ANY)] * len(results),
        out_specs=[hbm] * len(results),
        scratch_shapes=[dma((len(results),))],
        compiler_params=pltpu.CompilerParams(vmem_limit_bytes=8 * 1024 * 1024),
    )(*results)


def solution(mesh):
    in_specs = (
        P("seq", "tile"),
        P("seq", "tile"),
        P("seq", "tile"),
        P(None, None, "tile"),
        P(None, "tile"),
        P("tile", None),
        P("seq", "tile"),
    )
    out_specs = (
        P("seq", "tile"),
        P("seq", "tile"),
        P("seq", "tile"),
        P("seq", "tile"),
        P(None, None, "tile"),
        P(None, "tile"),
    )
    body = functools.partial(shards, mesh.shape["seq"], mesh.shape["tile"])
    return jax.shard_map(body, mesh=mesh, in_specs=in_specs, out_specs=out_specs, check_vma=False)
```

profile of v0, /device:TPU:0, one launch (start us, length us, event | category | flops | bytes accessed | tf_op | source)
XLA Modules:
  0.0 51.6 jit_solution(12817762929861025931)
XLA Ops:
  0.6 49.0 %shard_map.181 = (f32[192,1024]{1,0:T(8,128)S(1)}, f32[192,1024]{1,0:T(8,128)S(1)}, f32[192,1024]{1,0:T(8,128)S(1)}, f32[192,1024]{1,0:T(8,128)S(1)}, f32[3,7,10...) custom-call(f32[192,1024]{1,0:T(8,128)} %xq.1, f32[192,1024]{1,0:T(8,128)} %xk.1, f32[192,1024]{1,0:T(8,128)} %xv.1, ...), custom_call_target="tpu_custom_call" | custom-call | tf_op jit(solution)/shard_map/pallas_call | solution.py:485
  49.7 1.9 %shard_map.182 = (f32[192,1024]{1,0:T(8,128)}, f32[192,1024]{1,0:T(8,128)}, f32[192,1024]{1,0:T(8,128)}, f32[192,1024]{1,0:T(8,128)}, f32[3,7,1024]{2,1,0:T(8,128)}, /*index=5*/f32[128,1024]{1,0:T(8,128)}) custom-call(f32[192,1024]{1,0:T(8,128)S(1)} %get-tuple-element.12.refs_0_, f32[192,1024]{1,0:T(8,128)S(1)} %get-tuple-element.13.refs_1_, ...), custom_call_target="tpu_custom_call" | custom-call | tf_op jit(solution)/shard_map/pallas_call | solution.py:553
where the time goes:
time: 51.7 us; the launch traced here: 51.6 us
  Pallas kernels  51 us (99%)
  between operations  0.64 us (1%)
    pallas_call x1, Pallas kernels, shards(): pl.pallas_call(functools.partial(kernel, n_seq, n_tile, n_own, scale), ou...  49 us
    pallas_call x1, Pallas kernels, shards(): pl.pallas_call(write_results, out_shape=tuple((jax.ShapeDtypeStruct(r.sha...  1.92 us

commit v1 on v0

--- a/solution.py
+++ b/solution.py
@@ -83,7 +83,7 @@
     inv_head_in, inv_taps_in,
     out_ref, gq_ref, gk_ref, gv_ref, gs_ref, gm_ref,
     sf, mf, fw_taps, fw_tail, fw_head, fw_after, inv_tail, inv_head, inv_taps,
-    xe, wv, cotv, hspec, gspec, vspec, ks, vs, qs, gated, gg, gmix, ge, gout, part,
+    xe, wv, cotv, hspec, gspec, vspec, ks, vs, qs, gated, gg, gmix, mix, ge, gout, part,
     ghalo_s, ghalo_r, mhalo_s, mhalo_r, psend, precv, msend, mrecv, mall, ssend, srecv, sall,
     t_sem, x_sem, w_sem, c_sem, xh_ss, xh_rs, ca_ss, ca_rs, gh_ss, gh_rs, mh_ss, mh_rs,
     eh_ss, eh_rs, p_ss, p_rs, m_ss, m_rs, ma_ss, ma_rs, s_ss, s_rs, sa_ss, sa_rs,
@@ -137,6 +137,36 @@
         copy.start()
     own_cot = pltpu.make_async_copy(cot, cotv.at[0], c_sem)
     own_cot.start()
+    barrier = pltpu.get_barrier_semaphore()
+
+    def greet(d, carry):
+        pl.semaphore_signal(barrier, inc=1, device_id={"seq": (me + d) % n_seq}, device_id_type=MESH)
+        return carry
+    lax.fori_loop(1, n_seq, greet, 0)
+    for k in range(bits):
+        pl.semaphore_signal(barrier, inc=1, device_id={"tile": flip(k)}, device_id_type=MESH)
+    pl.semaphore_wait(barrier, n_seq - 1 + bits)
+
+    has_next = me < n_seq - 1
+    has_prev = me > 0
+    nxt = (me + 1) % n_seq
+    prv = (me + n_seq - 1) % n_seq
+
+    x_halo = [
+        to_seq(x_refs[i].at[pl.ds(rows - EDGE, EDGE)], xe.at[i, pl.ds(0, EDGE)], xh_ss.at[i], xh_rs.at[i], nxt)
+        for i in range(3)
+    ]
+
+    @pl.when(has_next)
+    def _():
+        for i in (1, 2, 0):
+            x_halo[i].start()
+
+    gather = {}
+    for k in reversed(range(bits)):
+        gather[1 << k] = to_tile(cot, cotv.at[1 << k], ca_ss.at[1 << k], ca_rs.at[1 << k], k)
+        gather[1 << k].start()
+
     for copy in tables[3:]:
         copy.start()
     w_copies = []
@@ -144,36 +174,6 @@
         columns = pl.ds(pl.multiple_of(relative(r) * block, block), block)
         w_copies.append(pltpu.make_async_copy(weight.at[:, columns], wv.at[r], w_sem.at[r]))
         w_copies[-1].start()
-
-    barrier = pltpu.get_barrier_semaphore()
-
-    def greet(d, carry):
-        pl.semaphore_signal(barrier, inc=1, device_id={"seq": (me + d) % n_seq}, device_id_type=MESH)
-        return carry
-    lax.fori_loop(1, n_seq, greet, 0)
-    for k in range(bits):
-        pl.semaphore_signal(barrier, inc=1, device_id={"tile": flip(k)}, device_id_type=MESH)
-    pl.semaphore_wait(barrier, n_seq - 1 + bits)
-
-    has_next = me < n_seq - 1
-    has_prev = me > 0
-    nxt = (me + 1) % n_seq
-    prv = (me + n_seq - 1) % n_seq
-
-    x_halo = [
-        to_seq(x_refs[i].at[pl.ds(rows - EDGE, EDGE)], xe.at[i, pl.ds(0, EDGE)], xh_ss.at[i], xh_rs.at[i], nxt)
-        for i in range(3)
-    ]
-
-    @pl.when(has_next)
-    def _():
-        for i in (1, 2, 0):
-            x_halo[i].start()
-
-    gather = {}
-    for k in reversed(range(bits)):
-        gather[1 << k] = to_tile(cot, cotv.at[1 << k], ca_ss.at[1 << k], ca_rs.at[1 << k], k)
-        gather[1 << k].start()
 
     @pl.when(jnp.logical_not(has_prev))
     def _():
@@ -225,65 +225,18 @@
     for copy in tables[3:]:
         copy.wait()
 
-    for r in range(n_tile):
-        if r == 0:
-            own_cot.wait()
-        else:
-            gather[r].wait_recv()
-            for k in reversed(range(low_bit(r))):
-                slot = r + (1 << k)
-                gather[slot] = to_tile(cotv.at[r], cotv.at[slot], ca_ss.at[slot], ca_rs.at[slot], k)
-                gather[slot].start()
-        w_copies[r].wait()
-
-        def grad_block(c, ls, r=r):
-            term = lax.dot_general(
-                cotv[r], wv[r, ls, :], (((1,), (1,)), ((), ())), preferred_element_type=F32
-            )
-            if r > 0:
-                term = term + gg[:, ls]
-            else:
-                gspec[:, ls] = dft_wide(fw_tail, gated[:, ls])
-                for sub in parts(c):
-                    qs[:, sub] = short_conv(0, sub)
-            gg[:, ls] = term
-            if r == n_tile - 1:
-                grad_mixed = term * qs[:, ls]
-                gmix[:, ls] = grad_mixed
-                mhalo_s[:, ls] = grad_mixed[:taps].astype(BF16)
-        over(WIDE, grad_block)
-
-    mhalo = to_seq(mhalo_s, mhalo_r, mh_ss, mh_rs, prv)
-
-    @pl.when(has_prev)
-    def _():
-        mhalo.start()
-
-    @pl.when(has_prev)
-    def _():
-        ghalo.wait_recv()
-
     per_wide = WIDE // LANES
 
     def mixed_rows(c, ls):
-        v_spec = dft_wide(fw_head, gmix[:, ls])
-        vspec[:, ls] = v_spec
         spectrum = gspec[:, ls] + dft_half(fw_taps, ghalo_r[:, ls])
+        gspec[:, ls] = spectrum
         mixed = dft_wide(inv_tail, times(spectrum, hspec[:, ls]))
+        mix[:, ls] = mixed
         gout[:, ls] = (qs[:, ls] * mixed).astype(BF16)
-        ge[0, pl.ds(0, rows), ls] = gg[:, ls] * mixed
-        terms = (dft_wide(inv_taps, conj_times(spectrum, v_spec)) * scale).astype(BF16)
-        for p in range(per_wide):
-            msend[c * per_wide + p] = terms[:, p * LANES:(p + 1) * LANES]
-    over(WIDE, mixed_rows)
 
     e_halo = [
         to_seq(ge.at[i, pl.ds(0, EDGE)], ge.at[i, pl.ds(rows, EDGE)], eh_ss.at[i], eh_rs.at[i], prv) for i in range(3)
     ]
-
-    @pl.when(has_prev)
-    def _():
-        e_halo[0].start()
 
     scatter = {}
 
@@ -348,8 +301,6 @@
 
     medium_set = (msend, mrecv, m_ss, m_rs, mall, ma_ss, ma_rs)
     short_set = (ssend, srecv, s_ss, s_rs, sall, sa_ss, sa_rs)
-    to_owners(*medium_set[:4])
-
     def add_sums(r, first, last):
         total = part[r]
         for k in range(first, last):
@@ -381,9 +332,70 @@
                 total = total + sf[i, pl.ds(j, 1), sub] * ge[i, pl.ds(j, rows), sub]
             outs[i][:, sub] = total
 
-    for r in range(n_tile - 1, 0, -2):
-        project(r, (lambda c, ls: short_grad(0, c)) if r == n_tile - 1 else None)
-        send_sum(r)
+    for r in range(n_tile):
+        if r == 0:
+            own_cot.wait()
+        else:
+            gather[r].wait_recv()
+            for k in reversed(range(low_bit(r))):
+                slot = r + (1 << k)
+                gather[slot] = to_tile(cotv.at[r], cotv.at[slot], ca_ss.at[slot], ca_rs.at[slot], k)
+                gather[slot].start()
+        if r < 2:
+            w_copies[r].wait()
+        if r == 2:
+            for even in range(2, n_tile, 2):
+                project(even)
+
+        def grad_block(c, ls, r=r):
+            term = lax.dot_general(
+                cotv[r], wv[r, ls, :], (((1,), (1,)), ((), ())), preferred_element_type=F32
+            )
+            if r > 0:
+                term = term + gg[:, ls]
+            else:
+                gspec[:, ls] = dft_wide(fw_tail, gated[:, ls])
+                for sub in parts(c):
+                    qs[:, sub] = short_conv(0, sub)
+            if r < n_tile - 1:
+                gg[:, ls] = term
+            else:
+                ge[0, pl.ds(0, rows), ls] = term * mix[:, ls]
+                grad_mixed = term * qs[:, ls]
+                gmix[:, ls] = grad_mixed
+                mhalo_s[:, ls] = grad_mixed[:taps].astype(BF16)
+        over(WIDE, grad_block)
+
+        if r == 1:
+            @pl.when(has_prev)
+            def _():
+                ghalo.wait_recv()
+            over(WIDE, mixed_rows)
+            for late in range(2, n_tile):
+                w_copies[late].wait()
+            for odd in range(n_tile - 1, 0, -2):
+                project(odd)
+                send_sum(odd)
+        if r == 2:
+            for k in range(1, bits):
+                step_sums(k)
+
+    mhalo = to_seq(mhalo_s, mhalo_r, mh_ss, mh_rs, prv)
+
+    @pl.when(has_prev)
+    def _():
+        mhalo.start()
+        e_halo[0].start()
+
+    def medium_grad(c, ls):
+        v_spec = dft_wide(fw_head, gmix[:, ls])
+        vspec[:, ls] = v_spec
+        terms = (dft_wide(inv_taps, conj_times(gspec[:, ls], v_spec)) * scale).astype(BF16)
+        for p in range(per_wide):
+            msend[c * per_wide + p] = terms[:, p * LANES:(p + 1) * LANES]
+    over(WIDE, medium_grad)
+    to_owners(*medium_set[:4])
+    project(0, lambda c, ls: short_grad(0, c))
 
     @pl.when(has_next)
     def _():
@@ -397,24 +409,20 @@
         ge[2, pl.ds(0, rows), ls] = grad_prod * ks[:, ls]
         feature_grad(0, c)
 
-    project(2 % n_tile, product_rows)
+    over(WIDE, product_rows)
 
     @pl.when(has_prev)
     def _():
         e_halo[1].start()
         e_halo[2].start()
 
-    for r in range(4, n_tile, 2):
-        project(r)
-    for k in range(1, bits):
-        step_sums(k)
     owner_sum(*medium_set)
 
     def last_short(c, ls):
         short_grad(1, c)
         short_grad(2, c)
 
-    project(0, last_short)
+    over(WIDE, last_short)
     to_owners(*short_set[:4])
 
     @pl.when(has_next)
@@ -504,6 +512,7 @@
             pltpu.VMEM((size, width), F32),
             pltpu.VMEM((size, width), F32),
             pltpu.VMEM((size, width), F32),
+            pltpu.VMEM((rows, width), F32),
             pltpu.VMEM((rows, width), F32),
             pltpu.VMEM((rows, width), F32),
             pltpu.VMEM((rows, width), F32),

time: 51.7 us -> 56.7 us (1.097)
  Pallas kernels: 51 us -> 55.9 us
    pallas_call x1, Pallas kernels: 49 us -> 54 us  [shards(): pl.pallas_call(functools.partial(kernel, n_seq, n_tile, n_own, scale), ou...]
where the time goes in v1:
time: 56.7 us; the launch traced here: 56.6 us
  Pallas kernels  55.9 us (99%)
  between operations  0.64 us (1%)
    pallas_call x1, Pallas kernels, shards(): pl.pallas_call(functools.partial(kernel, n_seq, n_tile, n_own, scale), ou...  54 us
    pallas_call x1, Pallas kernels, shards(): pl.pallas_call(write_results, out_shape=tuple((jax.ShapeDtypeStruct(r.sha...  1.92 us

profile of v1, /device:TPU:0, one launch (start us, length us, event | category | flops | bytes accessed | tf_op | source)
XLA Modules:
  0.0 56.6 jit_solution(2169763240508967210)
XLA Ops:
  0.6 54.0 %shard_map.181 = (f32[192,1024]{1,0:T(8,128)S(1)}, f32[192,1024]{1,0:T(8,128)S(1)}, f32[192,1024]{1,0:T(8,128)S(1)}, f32[192,1024]{1,0:T(8,128)S(1)}, f32[3,7,10...) custom-call(f32[192,1024]{1,0:T(8,128)} %xq.1, f32[192,1024]{1,0:T(8,128)} %xk.1, f32[192,1024]{1,0:T(8,128)} %xv.1, ...), custom_call_target="tpu_custom_call" | custom-call | tf_op jit(solution)/shard_map/pallas_call | solution.py:493
  54.7 1.9 %shard_map.182 = (f32[192,1024]{1,0:T(8,128)}, f32[192,1024]{1,0:T(8,128)}, f32[192,1024]{1,0:T(8,128)}, f32[192,1024]{1,0:T(8,128)}, f32[3,7,1024]{2,1,0:T(8,128)}, /*index=5*/f32[128,1024]{1,0:T(8,128)}) custom-call(f32[192,1024]{1,0:T(8,128)S(1)} %get-tuple-element.12.refs_0_, f32[192,1024]{1,0:T(8,128)S(1)} %get-tuple-element.13.refs_1_, ...), custom_call_target="tpu_custom_call" | custom-call | tf_op jit(solution)/shard_map/pallas_call | solution.py:562
